TPU v7x, 512 devices: a whole 4x4x16 slice. The times are simulated.
512 devices in a mesh: gx: 8 (over x, z_hi), gy: 4 (over y), gz: 16 (over z_lo, core).
Axes of the slice: x: 4, y: 4, z: 16 (z_hi: 2, z_lo: 8; z = z_hi * 8 + z_lo), core: 2. Of those that a mesh axis runs over, the one named last changes fastest.
Arguments:
- volume: float32 [128, 128, 1024], P('gz', 'gx', 'gy'), may hold values from -10 to 10
Outputs:
- diffused: float32 [128, 128, 1024], P('gz', 'gx', 'gy')
All inputs are finite; a program needn't handle non-finite values.
Results may differ from a plain program's by a relative error of at most 0.0003.
Values sent between devices are 32-bit elements; how exact they have to be, the bound alone decides.
A program may use at most 64 MiB of HBM per device.

v0:
```python
import jax
import jax.numpy as jnp
from jax import lax
from jax.sharding import PartitionSpec as P

kernel_taps = (0.41111229, 0.8007374, 1.0, 0.8007374, 0.41111229)
time_step = 3000.0
contrast = 0.1


def extended(shard, sides, width):
    for axis, dim in sides:
        peers, length = (lax.axis_size(axis), shard.shape[dim])
        up = [(i, (i + 1) % peers) for i in range(peers - 1)]
        down = [(j, i) for i, j in up]
        last = lax.slice_in_dim(shard, length - width, length, axis=dim)
        leading = lax.slice_in_dim(shard, 0, width, axis=dim)
        before = lax.ppermute(last, axis, up)
        after = lax.ppermute(leading, axis, down)
        shard = jnp.concatenate([before, shard, after], axis=dim)
    return shard


def blur_valid(values, first_dim):
    weight_sum = sum(kernel_taps)
    for axis_dim in range(first_dim, first_dim + 3):
        out_size = values.shape[axis_dim] - 4
        blurred = kernel_taps[0] / weight_sum * lax.slice_in_dim(values, 0, out_size, axis=axis_dim)
        for offset in range(1, 5):
            blurred = blurred + kernel_taps[offset] / weight_sum * lax.slice_in_dim(
                values, offset, offset + out_size, axis=axis_dim
            )
        values = blurred
    return values


def gradients(values, first_dim):
    result = []
    for axis_dim in range(first_dim, first_dim + 3):
        cropped = values
        for other_dim in range(first_dim, first_dim + 3):
            if other_dim != axis_dim:
                cropped = lax.slice_in_dim(cropped, 1, cropped.shape[other_dim] - 1, axis=other_dim)
        length = cropped.shape[axis_dim] - 2
        forward = lax.slice_in_dim(cropped, 2, length + 2, axis=axis_dim)
        behind = lax.slice_in_dim(cropped, 0, length, axis=axis_dim)
        result.append((forward - behind) * 0.5)
    return result


def shifted(values, stride, axis_dim, fill_value):
    length = values.shape[axis_dim]
    if abs(stride) >= length:
        return jnp.full(values.shape, fill_value, values.dtype)
    pad_shape = list(values.shape)
    pad_shape[axis_dim] = abs(stride)
    padding = jnp.full(tuple(pad_shape), fill_value, values.dtype)
    if stride > 0:
        return jnp.concatenate(
            [padding, lax.slice_in_dim(values, 0, length - stride, axis=axis_dim)], axis=axis_dim
        )
    return jnp.concatenate(
        [lax.slice_in_dim(values, -stride, length, axis=axis_dim), padding], axis=axis_dim
    )


def every_other(values, first_row, axis_dim):
    return lax.slice_in_dim(values, first_row, values.shape[axis_dim], stride=2, axis=axis_dim)


def reduce_solve(sub_diag, main_diag, super_diag, right_sides, axis_dim):
    length = main_diag.shape[axis_dim]
    if length == 1:
        return [right_side / main_diag for right_side in right_sides]
    even_sub = every_other(sub_diag, 0, axis_dim)
    odd_sub = every_other(sub_diag, 1, axis_dim)
    even_main = every_other(main_diag, 0, axis_dim)
    odd_main = every_other(main_diag, 1, axis_dim)
    even_super = every_other(super_diag, 0, axis_dim)
    odd_super = every_other(super_diag, 1, axis_dim)
    even_sides = [every_other(right_side, 0, axis_dim) for right_side in right_sides]
    odd_sides = [every_other(right_side, 1, axis_dim) for right_side in right_sides]
    lower_factor = -even_sub / shifted(odd_main, 1, axis_dim, 1.0)
    upper_factor = -even_super / odd_main
    reduced = reduce_solve(
        lower_factor * shifted(odd_sub, 1, axis_dim, 0.0),
        even_main + lower_factor * shifted(odd_super, 1, axis_dim, 0.0) + upper_factor * odd_sub,
        upper_factor * odd_super,
        [
            even_side + lower_factor * shifted(odd_side, 1, axis_dim, 0.0) + upper_factor * odd_side
            for even_side, odd_side in zip(even_sides, odd_sides)
        ],
        axis_dim,
    )
    result = []
    for even_part, odd_side in zip(reduced, odd_sides):
        odd_part = (
            odd_side - odd_sub * even_part - odd_super * shifted(even_part, -1, axis_dim, 0.0)
        ) / odd_main
        joined = jnp.stack([even_part, odd_part], axis=axis_dim + 1)
        joined_shape = list(even_part.shape)
        joined_shape[axis_dim] = 2 * joined_shape[axis_dim]
        result.append(joined.reshape(tuple(joined_shape)))
    return result


def face_pairs(diffusivity, axis_dim, position, device_count):
    cropped = diffusivity
    for other_dim in range(3):
        if other_dim != axis_dim:
            cropped = lax.slice_in_dim(cropped, 1, cropped.shape[other_dim] - 1, axis=other_dim)
    length = cropped.shape[axis_dim] - 2
    centre = lax.slice_in_dim(cropped, 1, length + 1, axis=axis_dim)
    following = lax.slice_in_dim(cropped, 2, length + 2, axis=axis_dim)
    before = lax.slice_in_dim(cropped, 0, length, axis=axis_dim)
    face_up = (centre + following) * 0.5
    face_down = (before + centre) * 0.5
    global_index = position * length + lax.broadcasted_iota(jnp.int32, face_up.shape, axis_dim)
    face_up = jnp.where(global_index < length * device_count - 1, face_up, 0.0)
    face_down = jnp.where(global_index > 0, face_down, 0.0)
    return (face_up, face_down)


def line_solve(values, face_up, axis_dim, stiffness):
    face_down = shifted(face_up, 1, axis_dim, 0.0)
    return reduce_solve(
        -stiffness * face_down,
        1.0 + stiffness * (face_down + face_up),
        -stiffness * face_up,
        [values],
        axis_dim,
    )[0]


def body(volume):
    stiffness = 3.0 * time_step
    positions = (lax.axis_index("gz"), lax.axis_index("gx"), lax.axis_index("gy"))
    counts = (lax.axis_size("gz"), lax.axis_size("gx"), lax.axis_size("gy"))
    widened = extended(volume, (("gx", 1), ("gy", 2), ("gz", 0)), 3)
    blurred = blur_valid(widened, 0)
    squares = jnp.stack([slope * slope for slope in gradients(blurred, 0)])
    square_halo = extended(squares, (("gx", 2), ("gy", 3), ("gz", 1)), 3)
    tensor = blur_valid(square_halo, 1)
    diffusivity = 1.0 / (1.0 + tensor / (contrast * contrast))
    up_z, down_z = face_pairs(diffusivity[0], 0, positions[0], counts[0])
    up_x, down_x = face_pairs(diffusivity[1], 1, positions[1], counts[1])
    up_y, down_y = face_pairs(diffusivity[2], 2, positions[2], counts[2])
    lines_x = (lambda pieces: line_solve(pieces[0], pieces[1], 1, stiffness))(
        (
            lax.all_to_all(volume, "gx", split_axis=0, concat_axis=1, tiled=True),
            lax.all_to_all(up_x, "gx", split_axis=0, concat_axis=1, tiled=True),
        )
    )
    solved_x = lax.all_to_all(lines_x, "gx", split_axis=1, concat_axis=0, tiled=True)
    lines_y = (lambda pieces: line_solve(pieces[0], pieces[1], 2, stiffness))(
        (
            lax.all_to_all(volume, "gy", split_axis=0, concat_axis=2, tiled=True),
            lax.all_to_all(up_y, "gy", split_axis=0, concat_axis=2, tiled=True),
        )
    )
    solved_y = lax.all_to_all(lines_y, "gy", split_axis=2, concat_axis=0, tiled=True)
    lines_z = (lambda pieces: line_solve(pieces[0], pieces[1], 0, stiffness))(
        (
            lax.all_to_all(volume, "gz", split_axis=1, concat_axis=0, tiled=True),
            lax.all_to_all(up_z, "gz", split_axis=1, concat_axis=0, tiled=True),
        )
    )
    solved_z = lax.all_to_all(lines_z, "gz", split_axis=0, concat_axis=1, tiled=True)
    summed = solved_x + solved_y + solved_z
    return summed / 3.0


def solution(mesh):
    return jax.shard_map(
        body,
        mesh=mesh,
        in_specs=(P("gz", "gx", "gy"),),
        out_specs=P("gz", "gx", "gy"),
        check_vma=False,
    )
```

profile of v0, /device:TPU:1, one launch (start us, length us, event | category | flops | bytes accessed | tf_op | source)
XLA Modules:
  0.0 376.5 jit_solution(18184623434700100287)
XLA Ops:
  2.4 16.3 %collective-permute-start = (f32[8,3,256]{2,0,1:T(8,128)S(1)}, f32[8,3,256]{2,0,1:T(8,128)S(1)}, u32[]{:S(2)}, u32[]{:S(2)}) collective-permute-start(f32[8,3,256]{2,0,1:T(8,128)S(1)} %get-tuple-element.90), channel_id=1, source_target_pairs={{0,64},{64,128},{128,192},{192,256},{256,320},{320,384},{384,448},... | collective-permute-start | bytes 73736 | tf_op jit(solution)/shard_map/ppermute | solution.py:18
  21.0 11.0 %collective-permute-done.1 = f32[8,3,256]{2,0,1:T(8,128)S(1)} collective-permute-done((f32[8,3,256]{2,0,1:T(8,128)S(1)}, f32[8,3,256]{2,0,1:T(8,128)S(1)}, u32[]{:S(2)}, u32[]{:S(2)}) %collective-permute-start.1) | collective-permute-done | bytes 24608 | tf_op jit(solution)/shard_map/ppermute | solution.py:19
  36.8 3.7 collective-permute-done.3
  40.7 6.1 %collective-permute-start.4 = (f32[3,22,262]{2,0,1:T(4,128)S(1)}, f32[3,22,262]{2,0,1:T(4,128)S(1)}, u32[]{:S(2)}, u32[]{:S(2)}) collective-permute-start(f32[3,22,262]{2,0,1:T(4,128)S(1)} %get-tuple-element.62), channel_id=1, source_target_pairs={{0,1},{1,2},{2,3},{3,4},{4,5},{5,6},{6,7},{7,8},{8,9},{9,10},{10,1... | collective-permute-start | bytes 207512 | tf_op jit(solution)/shard_map/ppermute | solution.py:18
  48.7 3.9 %all-to-all-start.3 = ((f32[8,16,256]{2,1,0:T(8,128)}), f32[8,16,256]{2,1,0:T(8,128)}, u32[]{:S(2)}, u32[]{:S(2)}) async-start(f32[8,16,256]{2,1,0:T(8,128)} %param.1), calls=%async_computation.3 | async-start | bytes 262144 | tf_op jit(solution)/shard_map/all_to_all | solution.py:157
  59.3 16.2 %collective-permute-done.7 = f32[3,8,3,256]{3,1,2,0:T(8,128)S(1)} collective-permute-done((f32[3,8,3,256]{3,1,2,0:T(8,128)S(1)}, f32[3,8,3,256]{3,1,2,0:T(8,128)S(1)}, u32[]{:S(2)}, u32[]{:S(2)}) %collective-permute-start.7) | collective-permute-done | bytes 73760 | tf_op jit(solution)/shard_map/ppermute | solution.py:19
  75.7 3.7 collective-permute-start.8
  80.7 4.4 %collective-permute-done.8 = f32[3,8,22,3]{3,1,2,0:T(8,128)S(1)} collective-permute-done((f32[3,8,22,3]{3,1,2,0:T(8,128)S(1)}, f32[3,8,22,3]{3,1,2,0:T(8,128)S(1)}, u32[]{:S(2)}, u32[]{:S(2)}) %collective-permute-start.8) | collective-permute-done | bytes 6368 | tf_op jit(solution)/shard_map/ppermute | solution.py:18
  85.1 3.8 %collective-permute-done.9 = f32[3,8,22,3]{3,1,2,0:T(8,128)S(1)} collective-permute-done((f32[3,8,22,3]{3,1,2,0:T(8,128)S(1)}, f32[3,8,22,3]{3,1,2,0:T(8,128)S(1)}, u32[]{:S(2)}, u32[]{:S(2)}) %collective-permute-start.9) | collective-permute-done | bytes 6368 | tf_op jit(solution)/shard_map/ppermute | solution.py:19
  90.3 10.5 %collective-permute-start.10 = (f32[3,3,22,262]{3,1,2,0:T(4,128)}, f32[3,3,22,262]{3,1,2,0:T(4,128)S(1)}, u32[]{:S(2)}, u32[]{:S(2)}) collective-permute-start(f32[3,3,22,262]{3,1,2,0:T(4,128)} %get-tuple-element.47), channel_id=1, source_target_pairs={{0,1},{1,2},{2,3},{3,4},{4,5},{5,6},{6,7},{7,8},{8,9},{9,10},{10,1... | collective-permute-start | bytes 622520 | tf_op jit(solution)/shard_map/ppermute | solution.py:18
  103.2 8.4 %all-to-all-start = ((f32[8,16,256]{2,1,0:T(8,128)}), f32[8,16,256]{2,1,0:T(8,128)}, u32[]{:S(2)}, u32[]{:S(2)}) async-start(f32[8,16,256]{2,1,0:T(8,128)} %param.1), calls=%async_computation | async-start | bytes 262144 | tf_op jit(solution)/shard_map/all_to_all | solution.py:150
  116.8 4.1 %slice.1277 = f32[2,16,512]{1,2,0:T(8,128)} slice(f32[2,16,1024]{1,2,0:T(8,128)} %bitcast.240), slice={[0:2:1], [0:16:1], [0:1024:2]} | slice | bytes 131072 | tf_op jit(solution)/shard_map/slice | solution.py:68
  120.9 3.7 maximum_maximum_fusion
  138.6 8.0 %all-to-all-start.6 = ((f32[8,16,256]{2,0,1:T(8,128)}), f32[8,16,256]{2,0,1:T(8,128)}, u32[]{:S(2)}, u32[]{:S(2)}) async-start(f32[8,16,256]{2,0,1:T(8,128)} %copy.184), calls=%async_computation.6 | async-start | bytes 262144 | tf_op jit(solution)/shard_map/all_to_all | solution.py:164
  151.5 4.1 %slice.1283 = f32[2,16,512]{1,2,0:T(8,128)} slice(f32[2,16,1024]{1,2,0:T(8,128)} %get-tuple-element.44), slice={[0:2:1], [0:16:1], [0:1024:2]} | slice | bytes 131072 | tf_op jit(solution)/shard_map/slice | solution.py:68
  158.5 4.1 %slice.1288 = f32[2,16,512]{1,2,0:T(8,128)} slice(f32[2,16,1024]{1,2,0:T(8,128)} %get-tuple-element.46), slice={[0:2:1], [0:16:1], [0:1024:2]} | slice | bytes 131072 | tf_op jit(solution)/shard_map/slice | solution.py:68
  276.0 14.1 %all-to-all-start.1 = ((f32[8,16,256]{2,1,0:T(8,128)}), f32[8,16,256]{2,1,0:T(8,128)S(1)}, u32[]{:S(2)}, u32[]{:S(2)}) async-start(f32[8,16,256]{2,1,0:T(8,128)} %copy.187), calls=%async_computation.1 | async-start | bytes 262144 | tf_op jit(solution)/shard_map/all_to_all | solution.py:151
  297.4 7.1 %all-to-all-done.1 = f32[8,16,256]{2,1,0:T(8,128)S(1)} async-done(((f32[8,16,256]{2,1,0:T(8,128)}), f32[8,16,256]{2,1,0:T(8,128)S(1)}, u32[]{:S(2)}, u32[]{:S(2)}) %all-to-all-start.1) | async-done | bytes 131104 | tf_op jit(solution)/shard_map/all_to_all | solution.py:151
  304.5 13.9 %all-to-all-start.7 = ((f32[8,16,256]{2,0,1:T(8,128)}), f32[8,16,256]{2,0,1:T(8,128)S(1)}, u32[]{:S(2)}, u32[]{:S(2)}) async-start(f32[8,16,256]{2,0,1:T(8,128)} %fusion.30), calls=%async_computation.7 | async-start | bytes 262144 | tf_op jit(solution)/shard_map/all_to_all | solution.py:165
  322.2 8.2 %all-to-all-done.7 = f32[8,16,256]{2,0,1:T(8,128)S(1)} async-done(((f32[8,16,256]{2,0,1:T(8,128)}), f32[8,16,256]{2,0,1:T(8,128)S(1)}, u32[]{:S(2)}, u32[]{:S(2)}) %all-to-all-start.7) | async-done | bytes 131104 | tf_op jit(solution)/shard_map/all_to_all | solution.py:165
  330.4 3.5 all-to-all-start.5
  342.9 13.4 %all-to-all-done.2 = f32[1,128,256]{2,0,1:T(1,128)S(1)} async-done(((f32[1,128,256]{2,0,1:T(1,128)}), f32[1,128,256]{2,0,1:T(1,128)S(1)}, u32[]{:S(2)}, u32[]{:S(2)}) %all-to-all-start.2) | async-done | bytes 131104 | tf_op jit(solution)/shard_map/all_to_all | solution.py:154
  356.3 7.4 %all-to-all-start.8 = ((f32[128,1,256]{2,1,0:T(1,128)}), f32[128,1,256]{2,1,0:T(1,128)S(1)}, u32[]{:S(2)}, u32[]{:S(2)}) async-start(f32[128,1,256]{2,1,0:T(1,128)} %bitcast.99), calls=%async_computation.8 | async-start | bytes 262144 | tf_op jit(solution)/shard_map/all_to_all | solution.py:168
  367.1 8.6 %all-to-all-done.8 = f32[128,1,256]{2,1,0:T(1,128)S(1)} async-done(((f32[128,1,256]{2,1,0:T(1,128)}), f32[128,1,256]{2,1,0:T(1,128)S(1)}, u32[]{:S(2)}, u32[]{:S(2)}) %all-to-all-start.8) | async-done | bytes 131104 | tf_op jit(solution)/shard_map/all_to_all | solution.py:168
  (386 shorter events, 186.5 us)
Async XLA Ops:
  2.4 17.6 %collective-permute-start = (f32[8,3,256]{2,0,1:T(8,128)S(1)}, f32[8,3,256]{2,0,1:T(8,128)S(1)}, u32[]{:S(2)}, u32[]{:S(2)}) collective-permute-start(f32[8,3,256]{2,0,1:T(8,128)S(1)} %get-tuple-element.90), channel_id=1, source_target_pairs={{0,64},{64,128},{128,192},{192,256},{256,320},{320,384},{384,448},... | collective-permute-start | bytes 73736 | tf_op jit(solution)/shard_map/ppermute | solution.py:18
  18.7 13.3 %collective-permute-start.1 = (f32[8,3,256]{2,0,1:T(8,128)S(1)}, f32[8,3,256]{2,0,1:T(8,128)S(1)}, u32[]{:S(2)}, u32[]{:S(2)}) collective-permute-start(f32[8,3,256]{2,0,1:T(8,128)S(1)} %get-tuple-element.89), channel_id=1, source_target_pairs={{64,0},{128,64},{192,128},{256,192},{320,256},{384,320},{448,384},... | collective-permute-start | bytes 73736 | tf_op jit(solution)/shard_map/ppermute | solution.py:19
  32.0 4.8 %collective-permute-start.2 = (f32[8,22,3]{2,0,1:T(8,128)S(1)}, f32[8,22,3]{2,0,1:T(8,128)S(1)}, u32[]{:S(2)}, u32[]{:S(2)}) collective-permute-start(f32[8,22,3]{2,0,1:T(8,128)S(1)} %get-tuple-element.70), channel_id=1, source_target_pairs={{0,16},{16,32},{32,48},{1,17},{17,33},{33,49},{2,18},{18,34},{34,5... | collective-permute-start | bytes 6344 | tf_op jit(solution)/shard_map/ppermute | solution.py:18
  35.3 5.3 %collective-permute-start.3 = (f32[8,22,3]{2,0,1:T(8,128)S(1)}, f32[8,22,3]{2,0,1:T(8,128)S(1)}, u32[]{:S(2)}, u32[]{:S(2)}) collective-permute-start(f32[8,22,3]{2,0,1:T(8,128)S(1)} %get-tuple-element.71), channel_id=1, source_target_pairs={{16,0},{32,16},{48,32},{17,1},{33,17},{49,33},{18,2},{34,18},{50,3... | collective-permute-start | bytes 6344 | tf_op jit(solution)/shard_map/ppermute | solution.py:19
  40.7 12.0 %collective-permute-start.4 = (f32[3,22,262]{2,0,1:T(4,128)S(1)}, f32[3,22,262]{2,0,1:T(4,128)S(1)}, u32[]{:S(2)}, u32[]{:S(2)}) collective-permute-start(f32[3,22,262]{2,0,1:T(4,128)S(1)} %get-tuple-element.62), channel_id=1, source_target_pairs={{0,1},{1,2},{2,3},{3,4},{4,5},{5,6},{6,7},{7,8},{8,9},{9,10},{10,1... | collective-permute-start | bytes 207512 | tf_op jit(solution)/shard_map/ppermute | solution.py:18
  46.8 6.3 %collective-permute-start.5 = (f32[3,22,262]{2,0,1:T(4,128)S(1)}, f32[3,22,262]{2,0,1:T(4,128)S(1)}, u32[]{:S(2)}, u32[]{:S(2)}) collective-permute-start(f32[3,22,262]{2,0,1:T(4,128)S(1)} %get-tuple-element.63), channel_id=1, source_target_pairs={{1,0},{2,1},{3,2},{4,3},{5,4},{6,5},{7,6},{8,7},{9,8},{10,9},{11,1... | collective-permute-start | bytes 207512 | tf_op jit(solution)/shard_map/ppermute | solution.py:19
  48.7 54.4 %all-to-all-start.3 = ((f32[8,16,256]{2,1,0:T(8,128)}), f32[8,16,256]{2,1,0:T(8,128)}, u32[]{:S(2)}, u32[]{:S(2)}) async-start(f32[8,16,256]{2,1,0:T(8,128)} %param.1), calls=%async_computation.3 | async-start | bytes 262144 | tf_op jit(solution)/shard_map/all_to_all | solution.py:157
  54.8 4.4 %collective-permute-start.6 = (f32[3,8,3,256]{3,1,2,0:T(8,128)S(1)}, f32[3,8,3,256]{3,1,2,0:T(8,128)S(1)}, u32[]{:S(2)}, u32[]{:S(2)}) collective-permute-start(f32[3,8,3,256]{3,1,2,0:T(8,128)S(1)} %get-tuple-element.58), channel_id=1, source_target_pairs={{0,64},{64,128},{128,192},{192,256},{256,320},{320,384},{384,448},... | collective-permute-start | bytes 221192 | tf_op jit(solution)/shard_map/ppermute | solution.py:18
  57.9 17.6 %collective-permute-start.7 = (f32[3,8,3,256]{3,1,2,0:T(8,128)S(1)}, f32[3,8,3,256]{3,1,2,0:T(8,128)S(1)}, u32[]{:S(2)}, u32[]{:S(2)}) collective-permute-start(f32[3,8,3,256]{3,1,2,0:T(8,128)S(1)} %get-tuple-element.59), channel_id=1, source_target_pairs={{64,0},{128,64},{192,128},{256,192},{320,256},{384,320},{448,384},... | collective-permute-start | bytes 221192 | tf_op jit(solution)/shard_map/ppermute | solution.py:19
  59.3 30.0 %copy-start.3 = (f32[3,8,3,256]{3,1,2,0:T(8,128)}, f32[3,8,3,256]{3,1,2,0:T(8,128)S(1)}, u32[]{:S(2)}) copy-start(f32[3,8,3,256]{3,1,2,0:T(8,128)S(1)} %collective-permute-done.6) | copy-start | bytes 221188
  75.7 9.4 %collective-permute-start.8 = (f32[3,8,22,3]{3,1,2,0:T(8,128)S(1)}, f32[3,8,22,3]{3,1,2,0:T(8,128)S(1)}, u32[]{:S(2)}, u32[]{:S(2)}) collective-permute-start(f32[3,8,22,3]{3,1,2,0:T(8,128)S(1)} %get-tuple-element.49), channel_id=1, source_target_pairs={{0,16},{16,32},{32,48},{1,17},{17,33},{33,49},{2,18},{18,34},{34,5... | collective-permute-start | bytes 19016 | tf_op jit(solution)/shard_map/ppermute | solution.py:18
  79.4 9.5 %collective-permute-start.9 = (f32[3,8,22,3]{3,1,2,0:T(8,128)S(1)}, f32[3,8,22,3]{3,1,2,0:T(8,128)S(1)}, u32[]{:S(2)}, u32[]{:S(2)}) collective-permute-start(f32[3,8,22,3]{3,1,2,0:T(8,128)S(1)} %get-tuple-element.50), channel_id=1, source_target_pairs={{16,0},{32,16},{48,32},{17,1},{33,17},{49,33},{18,2},{34,18},{50,3... | collective-permute-start | bytes 19016 | tf_op jit(solution)/shard_map/ppermute | solution.py:19
  90.3 30.6 %collective-permute-start.10 = (f32[3,3,22,262]{3,1,2,0:T(4,128)}, f32[3,3,22,262]{3,1,2,0:T(4,128)S(1)}, u32[]{:S(2)}, u32[]{:S(2)}) collective-permute-start(f32[3,3,22,262]{3,1,2,0:T(4,128)} %get-tuple-element.47), channel_id=1, source_target_pairs={{0,1},{1,2},{2,3},{3,4},{4,5},{5,6},{6,7},{7,8},{8,9},{9,10},{10,1... | collective-permute-start | bytes 622520 | tf_op jit(solution)/shard_map/ppermute | solution.py:18
  100.8 20.1 %collective-permute-start.11 = (f32[3,3,22,262]{3,1,2,0:T(4,128)}, f32[3,3,22,262]{3,1,2,0:T(4,128)}, u32[]{:S(2)}, u32[]{:S(2)}) collective-permute-start(f32[3,3,22,262]{3,1,2,0:T(4,128)} %get-tuple-element.48), channel_id=1, source_target_pairs={{1,0},{2,1},{3,2},{4,3},{5,4},{6,5},{7,6},{8,7},{9,8},{10,9},{11,1... | collective-permute-start | bytes 622520 | tf_op jit(solution)/shard_map/ppermute | solution.py:19
  103.2 27.3 %all-to-all-start = ((f32[8,16,256]{2,1,0:T(8,128)}), f32[8,16,256]{2,1,0:T(8,128)}, u32[]{:S(2)}, u32[]{:S(2)}) async-start(f32[8,16,256]{2,1,0:T(8,128)} %param.1), calls=%async_computation | async-start | bytes 262144 | tf_op jit(solution)/shard_map/all_to_all | solution.py:150
  130.4 8.1 %all-to-all-start.4 = ((f32[8,16,256]{2,1,0:T(8,128)}), f32[8,16,256]{2,1,0:T(8,128)S(1)}, u32[]{:S(2)}, u32[]{:S(2)}) async-start(f32[8,16,256]{2,1,0:T(8,128)} %copy.189), calls=%async_computation.4 | async-start | bytes 262144 | tf_op jit(solution)/shard_map/all_to_all | solution.py:158
  138.6 137.4 %all-to-all-start.6 = ((f32[8,16,256]{2,0,1:T(8,128)}), f32[8,16,256]{2,0,1:T(8,128)}, u32[]{:S(2)}, u32[]{:S(2)}) async-start(f32[8,16,256]{2,0,1:T(8,128)} %copy.184), calls=%async_computation.6 | async-start | bytes 262144 | tf_op jit(solution)/shard_map/all_to_all | solution.py:164
  276.0 28.5 %all-to-all-start.1 = ((f32[8,16,256]{2,1,0:T(8,128)}), f32[8,16,256]{2,1,0:T(8,128)S(1)}, u32[]{:S(2)}, u32[]{:S(2)}) async-start(f32[8,16,256]{2,1,0:T(8,128)} %copy.187), calls=%async_computation.1 | async-start | bytes 262144 | tf_op jit(solution)/shard_map/all_to_all | solution.py:151
  293.5 25.4 %copy-start.2 = (f32[1,128,256]{2,0,1:T(1,128)S(1)}, f32[1,128,256]{2,0,1:T(1,128)}, u32[]{:S(2)}) copy-start(f32[1,128,256]{2,0,1:T(1,128)} %copy-done.1) | copy-start | bytes 393220
  293.5 25.4 %slice-start = ((f32[1,64,256]{2,0,1:T(1,128)}), f32[1,63,256]{2,0,1:T(1,128)S(1)}, s32[]{:S(2)}) async-start(f32[1,64,256]{2,0,1:T(1,128)} %copy-done.7), calls=%async_computation.9 | async-start | bytes 129024 | tf_op jit(solution)/shard_map/slice | solution.py:60
  304.5 25.9 %all-to-all-start.7 = ((f32[8,16,256]{2,0,1:T(8,128)}), f32[8,16,256]{2,0,1:T(8,128)S(1)}, u32[]{:S(2)}, u32[]{:S(2)}) async-start(f32[8,16,256]{2,0,1:T(8,128)} %fusion.30), calls=%async_computation.7 | async-start | bytes 262144 | tf_op jit(solution)/shard_map/all_to_all | solution.py:165
  330.4 8.1 %all-to-all-start.5 = ((f32[4,1,8192]{2,1,0:T(1,128)}), f32[4,1,8192]{2,1,0:T(1,128)S(1)}, u32[]{:S(2)}, u32[]{:S(2)}) async-start(f32[4,1,8192]{2,1,0:T(1,128)} %reshape.133), calls=%async_computation.5 | async-start | bytes 262144 | tf_op jit(solution)/shard_map/all_to_all | solution.py:161
  338.5 17.8 %all-to-all-start.2 = ((f32[1,128,256]{2,0,1:T(1,128)}), f32[1,128,256]{2,0,1:T(1,128)S(1)}, u32[]{:S(2)}, u32[]{:S(2)}) async-start(f32[1,128,256]{2,0,1:T(1,128)} %bitcast.24), calls=%async_computation.2 | async-start | bytes 262144 | tf_op jit(solution)/shard_map/all_to_all | solution.py:154
  356.3 19.4 %all-to-all-start.8 = ((f32[128,1,256]{2,1,0:T(1,128)}), f32[128,1,256]{2,1,0:T(1,128)S(1)}, u32[]{:S(2)}, u32[]{:S(2)}) async-start(f32[128,1,256]{2,1,0:T(1,128)} %bitcast.99), calls=%async_computation.8 | async-start | bytes 262144 | tf_op jit(solution)/shard_map/all_to_all | solution.py:168
  (6 other events, 52.7 us)
where the time goes:
time: 382 us; the launch traced here: 376 us
  local copies, waits for them, and re-layouts  132 us (35%)
  starting transfers between devices  118 us (31%)
  waiting for transfers between devices  82.8 us (22%)
  other arithmetic  41.6 us (11%)
    slice x133, local copies, waits for them, and re-layouts, every_other(): lax.slice_in_dim(values, first_row, values.shape[axis_dim], stride=2, axi...  112 us
    ppermute x6, starting transfers between devices, extended(): before = lax.ppermute(last, axis, up)  42.8 us
    ppermute x6, waiting for transfers between devices, extended(): after = lax.ppermute(leading, axis, down)  35.1 us
    add x21, other arithmetic, reduce_solve(): even_side + lower_factor * shifted(odd_side, 1, axis_dim, 0.0)  16.7 us
    all_to_all x1, starting transfers between devices, body(): lax.all_to_all(up_x, 'gx', split_axis=0, concat_axis=1, tiled=True)  14.1 us
    all_to_all x1, starting transfers between devices, body(): lax.all_to_all(up_z, 'gz', split_axis=1, concat_axis=0, tiled=True)  13.9 us
    all_to_all x1, waiting for transfers between devices, body(): lax.all_to_all(lines_x, 'gx', split_axis=1, concat_axis=0, tiled=True)  13.4 us
    ppermute x6, starting transfers between devices, extended(): after = lax.ppermute(leading, axis, down)  9.01 us
  transfers between devices with their start and end apart: 21, of which 14 were waited for; matrix products, arithmetic and copies ran while one was open for 45% of the time, Pallas kernels for 0%

commit v1 on v0

--- a/solution.py
+++ b/solution.py
@@ -158,7 +158,8 @@
             lax.all_to_all(up_y, "gy", split_axis=0, concat_axis=2, tiled=True),
         )
     )
-    solved_y = lax.all_to_all(lines_y, "gy", split_axis=2, concat_axis=0, tiled=True)
+    h_now = lax.all_to_all(jnp.stack(jnp.split(lines_y, lax.axis_size("gy"), 2)), "gy", 0, 0)
+    solved_y = jnp.concatenate(h_now, 0)
     lines_z = (lambda pieces: line_solve(pieces[0], pieces[1], 0, stiffness))(
         (
             lax.all_to_all(volume, "gz", split_axis=1, concat_axis=0, tiled=True),

time: 382 us -> 377 us (0.987)
  local copies, waits for them, and re-layouts: 132 us -> 124 us
  waiting for transfers between devices: 82.8 us -> 88.6 us
  transfers between devices with their start and end apart: 21 -> 21, of which waited for: 14 -> 14; matrix products, arithmetic and copies ran while one was open for 45% -> 43% of each run, Pallas kernels for 0% -> 0%
where the time goes in v1:
time: 377 us; the launch traced here: 372 us
  local copies, waits for them, and re-layouts  124 us (33%)
  starting transfers between devices  117 us (31%)
  waiting for transfers between devices  88.6 us (24%)
  other arithmetic  40.8 us (11%)
    slice x133, local copies, waits for them, and re-layouts, every_other(): lax.slice_in_dim(values, first_row, values.shape[axis_dim], stride=2, axi...  109 us
    ppermute x6, starting transfers between devices, extended(): before = lax.ppermute(last, axis, up)  42.9 us
    ppermute x6, waiting for transfers between devices, extended(): after = lax.ppermute(leading, axis, down)  35.2 us
    add x21, other arithmetic, reduce_solve(): even_side + lower_factor * shifted(odd_side, 1, axis_dim, 0.0)  16.7 us
    all_to_all x1, starting transfers between devices, body(): lax.all_to_all(up_x, 'gx', split_axis=0, concat_axis=1, tiled=True)  14.1 us
    all_to_all x1, starting transfers between devices, body(): lax.all_to_all(up_z, 'gz', split_axis=1, concat_axis=0, tiled=True)  13.9 us
    all_to_all x1, waiting for transfers between devices, body(): lax.all_to_all(lines_x, 'gx', split_axis=1, concat_axis=0, tiled=True)  11.5 us
    all_to_all x1, waiting for transfers between devices, body(): lax.all_to_all(up_x, 'gx', split_axis=0, concat_axis=1, tiled=True)  10.7 us
  transfers between devices with their start and end apart: 21, of which 14 were waited for; matrix products, arithmetic and copies ran while one was open for 43% of the time, Pallas kernels for 0%

profile of v1, /device:TPU:1, one launch (start us, length us, event | category | flops | bytes accessed | tf_op | source)
XLA Modules:
  0.0 371.8 jit_solution(5322520439602190186)
XLA Ops:
  2.4 16.3 %collective-permute-start = (f32[8,3,256]{2,0,1:T(8,128)S(1)}, f32[8,3,256]{2,0,1:T(8,128)S(1)}, u32[]{:S(2)}, u32[]{:S(2)}) collective-permute-start(f32[8,3,256]{2,0,1:T(8,128)S(1)} %get-tuple-element.94), channel_id=1, source_target_pairs={{0,64},{64,128},{128,192},{192,256},{256,320},{320,384},{384,448},... | collective-permute-start | bytes 73736 | tf_op jit(solution)/shard_map/ppermute | solution.py:18
  21.0 11.0 %collective-permute-done.1 = f32[8,3,256]{2,0,1:T(8,128)S(1)} collective-permute-done((f32[8,3,256]{2,0,1:T(8,128)S(1)}, f32[8,3,256]{2,0,1:T(8,128)S(1)}, u32[]{:S(2)}, u32[]{:S(2)}) %collective-permute-start.1) | collective-permute-done | bytes 24608 | tf_op jit(solution)/shard_map/ppermute | solution.py:19
  36.8 3.7 %collective-permute-done.3 = f32[8,22,3]{2,0,1:T(8,128)S(1)} collective-permute-done((f32[8,22,3]{2,0,1:T(8,128)S(1)}, f32[8,22,3]{2,0,1:T(8,128)S(1)}, u32[]{:S(2)}, u32[]{:S(2)}) %collective-permute-start.3) | collective-permute-done | bytes 2144 | tf_op jit(solution)/shard_map/ppermute | solution.py:19
  40.7 6.1 %collective-permute-start.4 = (f32[3,22,262]{2,0,1:T(4,128)S(1)}, f32[3,22,262]{2,0,1:T(4,128)S(1)}, u32[]{:S(2)}, u32[]{:S(2)}) collective-permute-start(f32[3,22,262]{2,0,1:T(4,128)S(1)} %get-tuple-element.66), channel_id=1, source_target_pairs={{0,1},{1,2},{2,3},{3,4},{4,5},{5,6},{6,7},{7,8},{8,9},{9,10},{10,1... | collective-permute-start | bytes 207512 | tf_op jit(solution)/shard_map/ppermute | solution.py:18
  48.7 3.9 %all-to-all-start.3 = ((f32[8,16,256]{2,1,0:T(8,128)}), f32[8,16,256]{2,1,0:T(8,128)S(1)}, u32[]{:S(2)}, u32[]{:S(2)}) async-start(f32[8,16,256]{2,1,0:T(8,128)} %param.1), calls=%async_computation.3 | async-start | bytes 262144 | tf_op jit(solution)/shard_map/all_to_all | solution.py:157
  59.3 16.2 %collective-permute-done.7 = f32[3,8,3,256]{3,1,2,0:T(8,128)S(1)} collective-permute-done((f32[3,8,3,256]{3,1,2,0:T(8,128)S(1)}, f32[3,8,3,256]{3,1,2,0:T(8,128)S(1)}, u32[]{:S(2)}, u32[]{:S(2)}) %collective-permute-start.7) | collective-permute-done | bytes 73760 | tf_op jit(solution)/shard_map/ppermute | solution.py:19
  75.7 3.7 %collective-permute-start.8 = (f32[3,8,22,3]{3,1,2,0:T(8,128)S(1)}, f32[3,8,22,3]{3,1,2,0:T(8,128)S(1)}, u32[]{:S(2)}, u32[]{:S(2)}) collective-permute-start(f32[3,8,22,3]{3,1,2,0:T(8,128)S(1)} %get-tuple-element.53), channel_id=1, source_target_pairs={{0,16},{16,32},{32,48},{1,17},{17,33},{33,49},{2,18},{18,34},{34,5... | collective-permute-start | bytes 19016 | tf_op jit(solution)/shard_map/ppermute | solution.py:18
  80.7 4.3 %collective-permute-done.8 = f32[3,8,22,3]{3,1,2,0:T(8,128)S(1)} collective-permute-done((f32[3,8,22,3]{3,1,2,0:T(8,128)S(1)}, f32[3,8,22,3]{3,1,2,0:T(8,128)S(1)}, u32[]{:S(2)}, u32[]{:S(2)}) %collective-permute-start.8) | collective-permute-done | bytes 6368 | tf_op jit(solution)/shard_map/ppermute | solution.py:18
  85.0 3.8 %collective-permute-done.9 = f32[3,8,22,3]{3,1,2,0:T(8,128)S(1)} collective-permute-done((f32[3,8,22,3]{3,1,2,0:T(8,128)S(1)}, f32[3,8,22,3]{3,1,2,0:T(8,128)S(1)}, u32[]{:S(2)}, u32[]{:S(2)}) %collective-permute-start.9) | collective-permute-done | bytes 6368 | tf_op jit(solution)/shard_map/ppermute | solution.py:19
  90.2 10.6 %collective-permute-start.10 = (f32[3,3,22,262]{3,1,2,0:T(4,128)}, f32[3,3,22,262]{3,1,2,0:T(4,128)}, u32[]{:S(2)}, u32[]{:S(2)}) collective-permute-start(f32[3,3,22,262]{3,1,2,0:T(4,128)} %get-tuple-element.51), channel_id=1, source_target_pairs={{0,1},{1,2},{2,3},{3,4},{4,5},{5,6},{6,7},{7,8},{8,9},{9,10},{10,1... | collective-permute-start | bytes 622520 | tf_op jit(solution)/shard_map/ppermute | solution.py:18
  103.1 8.4 %all-to-all-start = ((f32[8,16,256]{2,1,0:T(8,128)}), f32[8,16,256]{2,1,0:T(8,128)S(1)}, u32[]{:S(2)}, u32[]{:S(2)}) async-start(f32[8,16,256]{2,1,0:T(8,128)} %param.1), calls=%async_computation | async-start | bytes 262144 | tf_op jit(solution)/shard_map/all_to_all | solution.py:150
  115.9 4.1 %slice.1277 = f32[2,16,512]{1,2,0:T(8,128)} slice(f32[2,16,1024]{1,2,0:T(8,128)} %bitcast.242), slice={[0:2:1], [0:16:1], [0:1024:2]} | slice | bytes 131072 | tf_op jit(solution)/shard_map/slice | solution.py:68
  134.0 3.7 %all-to-all-done.4 = f32[8,16,256]{2,1,0:T(8,128)S(1)} async-done(((f32[8,16,256]{2,1,0:T(8,128)}), f32[8,16,256]{2,1,0:T(8,128)S(1)}, u32[]{:S(2)}, u32[]{:S(2)}) %all-to-all-start.4) | async-done | bytes 131104 | tf_op jit(solution)/shard_map/all_to_all | solution.py:158
  137.8 8.0 %all-to-all-start.6 = ((f32[8,16,256]{2,0,1:T(8,128)}), f32[8,16,256]{2,0,1:T(8,128)}, u32[]{:S(2)}, u32[]{:S(2)}) async-start(f32[8,16,256]{2,0,1:T(8,128)} %copy.184), calls=%async_computation.6 | async-start | bytes 262144 | tf_op jit(solution)/shard_map/all_to_all | solution.py:165
  150.7 4.1 %slice.1283 = f32[2,16,512]{1,2,0:T(8,128)} slice(f32[2,16,1024]{1,2,0:T(8,128)} %get-tuple-element.48), slice={[0:2:1], [0:16:1], [0:1024:2]} | slice | bytes 131072 | tf_op jit(solution)/shard_map/slice | solution.py:68
  157.8 4.1 %slice.1288 = f32[2,16,512]{1,2,0:T(8,128)} slice(f32[2,16,1024]{1,2,0:T(8,128)} %get-tuple-element.50), slice={[0:2:1], [0:16:1], [0:1024:2]} | slice | bytes 131072 | tf_op jit(solution)/shard_map/slice | solution.py:68
  272.2 14.1 %all-to-all-start.1 = ((f32[8,16,256]{2,1,0:T(8,128)}), f32[8,16,256]{2,1,0:T(8,128)S(1)}, u32[]{:S(2)}, u32[]{:S(2)}) async-start(f32[8,16,256]{2,1,0:T(8,128)} %copy.187), calls=%async_computation.1 | async-start | bytes 262144 | tf_op jit(solution)/shard_map/all_to_all | solution.py:151
  290.0 10.7 %all-to-all-done.1 = f32[8,16,256]{2,1,0:T(8,128)S(1)} async-done(((f32[8,16,256]{2,1,0:T(8,128)}), f32[8,16,256]{2,1,0:T(8,128)S(1)}, u32[]{:S(2)}, u32[]{:S(2)}) %all-to-all-start.1) | async-done | bytes 131104 | tf_op jit(solution)/shard_map/all_to_all | solution.py:151
  300.7 13.9 %all-to-all-start.7 = ((f32[8,16,256]{2,0,1:T(8,128)}), f32[8,16,256]{2,0,1:T(8,128)S(1)}, u32[]{:S(2)}, u32[]{:S(2)}) async-start(f32[8,16,256]{2,0,1:T(8,128)} %fusion.30), calls=%async_computation.7 | async-start | bytes 262144 | tf_op jit(solution)/shard_map/all_to_all | solution.py:166
  318.4 8.2 %all-to-all-done.7 = f32[8,16,256]{2,0,1:T(8,128)S(1)} async-done(((f32[8,16,256]{2,0,1:T(8,128)}), f32[8,16,256]{2,0,1:T(8,128)S(1)}, u32[]{:S(2)}, u32[]{:S(2)}) %all-to-all-start.7) | async-done | bytes 131104 | tf_op jit(solution)/shard_map/all_to_all | solution.py:166
  332.7 11.5 %all-to-all-done.2 = f32[1,128,256]{2,0,1:T(1,128)S(1)} async-done(((f32[1,128,256]{2,0,1:T(1,128)}), f32[1,128,256]{2,0,1:T(1,128)S(1)}, u32[]{:S(2)}, u32[]{:S(2)}) %all-to-all-start.2) | async-done | bytes 131104 | tf_op jit(solution)/shard_map/all_to_all | solution.py:154
  344.2 6.7 %all-to-all-start.8 = ((f32[128,1,256]{2,1,0:T(1,128)}), f32[128,1,256]{2,1,0:T(1,128)S(1)}, u32[]{:S(2)}, u32[]{:S(2)}) async-start(f32[128,1,256]{2,1,0:T(1,128)} %bitcast.101), calls=%async_computation.8 | async-start | bytes 262144 | tf_op jit(solution)/shard_map/all_to_all | solution.py:169
  353.0 10.0 %all-to-all-done.8 = f32[128,1,256]{2,1,0:T(1,128)S(1)} async-done(((f32[128,1,256]{2,1,0:T(1,128)}), f32[128,1,256]{2,1,0:T(1,128)S(1)}, u32[]{:S(2)}, u32[]{:S(2)}) %all-to-all-start.8) | async-done | bytes 131104 | tf_op jit(solution)/shard_map/all_to_all | solution.py:169
  366.3 4.8 %all-to-all-done.5 = f32[4,2,16,256]{3,2,1,0:T(8,128)S(1)} async-done(((f32[4,2,16,256]{3,2,1,0:T(8,128)}), f32[4,2,16,256]{3,2,1,0:T(8,128)S(1)}, u32[]{:S(2)}, u32[]{:S(2)}) %all-to-all-start.5) | async-done | bytes 131104 | tf_op jit(solution)/shard_map/all_to_all | solution.py:161
  (377 shorter events, 178.2 us)
Async XLA Ops:
  2.4 17.6 %collective-permute-start = (f32[8,3,256]{2,0,1:T(8,128)S(1)}, f32[8,3,256]{2,0,1:T(8,128)S(1)}, u32[]{:S(2)}, u32[]{:S(2)}) collective-permute-start(f32[8,3,256]{2,0,1:T(8,128)S(1)} %get-tuple-element.94), channel_id=1, source_target_pairs={{0,64},{64,128},{128,192},{192,256},{256,320},{320,384},{384,448},... | collective-permute-start | bytes 73736 | tf_op jit(solution)/shard_map/ppermute | solution.py:18
  18.7 13.3 %collective-permute-start.1 = (f32[8,3,256]{2,0,1:T(8,128)S(1)}, f32[8,3,256]{2,0,1:T(8,128)S(1)}, u32[]{:S(2)}, u32[]{:S(2)}) collective-permute-start(f32[8,3,256]{2,0,1:T(8,128)S(1)} %get-tuple-element.93), channel_id=1, source_target_pairs={{64,0},{128,64},{192,128},{256,192},{320,256},{384,320},{448,384},... | collective-permute-start | bytes 73736 | tf_op jit(solution)/shard_map/ppermute | solution.py:19
  32.0 4.8 %collective-permute-start.2 = (f32[8,22,3]{2,0,1:T(8,128)S(1)}, f32[8,22,3]{2,0,1:T(8,128)S(1)}, u32[]{:S(2)}, u32[]{:S(2)}) collective-permute-start(f32[8,22,3]{2,0,1:T(8,128)S(1)} %get-tuple-element.74), channel_id=1, source_target_pairs={{0,16},{16,32},{32,48},{1,17},{17,33},{33,49},{2,18},{18,34},{34,5... | collective-permute-start | bytes 6344 | tf_op jit(solution)/shard_map/ppermute | solution.py:18
  35.2 5.3 %collective-permute-start.3 = (f32[8,22,3]{2,0,1:T(8,128)S(1)}, f32[8,22,3]{2,0,1:T(8,128)S(1)}, u32[]{:S(2)}, u32[]{:S(2)}) collective-permute-start(f32[8,22,3]{2,0,1:T(8,128)S(1)} %get-tuple-element.75), channel_id=1, source_target_pairs={{16,0},{32,16},{48,32},{17,1},{33,17},{49,33},{18,2},{34,18},{50,3... | collective-permute-start | bytes 6344 | tf_op jit(solution)/shard_map/ppermute | solution.py:19
  40.7 11.9 %collective-permute-start.4 = (f32[3,22,262]{2,0,1:T(4,128)S(1)}, f32[3,22,262]{2,0,1:T(4,128)S(1)}, u32[]{:S(2)}, u32[]{:S(2)}) collective-permute-start(f32[3,22,262]{2,0,1:T(4,128)S(1)} %get-tuple-element.66), channel_id=1, source_target_pairs={{0,1},{1,2},{2,3},{3,4},{4,5},{5,6},{6,7},{7,8},{8,9},{9,10},{10,1... | collective-permute-start | bytes 207512 | tf_op jit(solution)/shard_map/ppermute | solution.py:18
  46.8 6.3 %collective-permute-start.5 = (f32[3,22,262]{2,0,1:T(4,128)S(1)}, f32[3,22,262]{2,0,1:T(4,128)S(1)}, u32[]{:S(2)}, u32[]{:S(2)}) collective-permute-start(f32[3,22,262]{2,0,1:T(4,128)S(1)} %get-tuple-element.67), channel_id=1, source_target_pairs={{1,0},{2,1},{3,2},{4,3},{5,4},{6,5},{7,6},{8,7},{9,8},{10,9},{11,1... | collective-permute-start | bytes 207512 | tf_op jit(solution)/shard_map/ppermute | solution.py:19
  48.7 54.4 %all-to-all-start.3 = ((f32[8,16,256]{2,1,0:T(8,128)}), f32[8,16,256]{2,1,0:T(8,128)S(1)}, u32[]{:S(2)}, u32[]{:S(2)}) async-start(f32[8,16,256]{2,1,0:T(8,128)} %param.1), calls=%async_computation.3 | async-start | bytes 262144 | tf_op jit(solution)/shard_map/all_to_all | solution.py:157
  54.9 4.4 %collective-permute-start.6 = (f32[3,8,3,256]{3,1,2,0:T(8,128)S(1)}, f32[3,8,3,256]{3,1,2,0:T(8,128)S(1)}, u32[]{:S(2)}, u32[]{:S(2)}) collective-permute-start(f32[3,8,3,256]{3,1,2,0:T(8,128)S(1)} %get-tuple-element.62), channel_id=1, source_target_pairs={{0,64},{64,128},{128,192},{192,256},{256,320},{320,384},{384,448},... | collective-permute-start | bytes 221192 | tf_op jit(solution)/shard_map/ppermute | solution.py:18
  57.9 17.6 %collective-permute-start.7 = (f32[3,8,3,256]{3,1,2,0:T(8,128)S(1)}, f32[3,8,3,256]{3,1,2,0:T(8,128)S(1)}, u32[]{:S(2)}, u32[]{:S(2)}) collective-permute-start(f32[3,8,3,256]{3,1,2,0:T(8,128)S(1)} %get-tuple-element.63), channel_id=1, source_target_pairs={{64,0},{128,64},{192,128},{256,192},{320,256},{384,320},{448,384},... | collective-permute-start | bytes 221192 | tf_op jit(solution)/shard_map/ppermute | solution.py:19
  75.7 9.3 %collective-permute-start.8 = (f32[3,8,22,3]{3,1,2,0:T(8,128)S(1)}, f32[3,8,22,3]{3,1,2,0:T(8,128)S(1)}, u32[]{:S(2)}, u32[]{:S(2)}) collective-permute-start(f32[3,8,22,3]{3,1,2,0:T(8,128)S(1)} %get-tuple-element.53), channel_id=1, source_target_pairs={{0,16},{16,32},{32,48},{1,17},{17,33},{33,49},{2,18},{18,34},{34,5... | collective-permute-start | bytes 19016 | tf_op jit(solution)/shard_map/ppermute | solution.py:18
  79.4 9.4 %collective-permute-start.9 = (f32[3,8,22,3]{3,1,2,0:T(8,128)S(1)}, f32[3,8,22,3]{3,1,2,0:T(8,128)S(1)}, u32[]{:S(2)}, u32[]{:S(2)}) collective-permute-start(f32[3,8,22,3]{3,1,2,0:T(8,128)S(1)} %get-tuple-element.54), channel_id=1, source_target_pairs={{16,0},{32,16},{48,32},{17,1},{33,17},{49,33},{18,2},{34,18},{50,3... | collective-permute-start | bytes 19016 | tf_op jit(solution)/shard_map/ppermute | solution.py:19
  90.2 29.8 %collective-permute-start.10 = (f32[3,3,22,262]{3,1,2,0:T(4,128)}, f32[3,3,22,262]{3,1,2,0:T(4,128)}, u32[]{:S(2)}, u32[]{:S(2)}) collective-permute-start(f32[3,3,22,262]{3,1,2,0:T(4,128)} %get-tuple-element.51), channel_id=1, source_target_pairs={{0,1},{1,2},{2,3},{3,4},{4,5},{5,6},{6,7},{7,8},{8,9},{9,10},{10,1... | collective-permute-start | bytes 622520 | tf_op jit(solution)/shard_map/ppermute | solution.py:18
  100.8 19.2 %collective-permute-start.11 = (f32[3,3,22,262]{3,1,2,0:T(4,128)}, f32[3,3,22,262]{3,1,2,0:T(4,128)}, u32[]{:S(2)}, u32[]{:S(2)}) collective-permute-start(f32[3,3,22,262]{3,1,2,0:T(4,128)} %get-tuple-element.52), channel_id=1, source_target_pairs={{1,0},{2,1},{3,2},{4,3},{5,4},{6,5},{7,6},{8,7},{9,8},{10,9},{11,1... | collective-permute-start | bytes 622520 | tf_op jit(solution)/shard_map/ppermute | solution.py:19
  103.1 26.5 %all-to-all-start = ((f32[8,16,256]{2,1,0:T(8,128)}), f32[8,16,256]{2,1,0:T(8,128)S(1)}, u32[]{:S(2)}, u32[]{:S(2)}) async-start(f32[8,16,256]{2,1,0:T(8,128)} %param.1), calls=%async_computation | async-start | bytes 262144 | tf_op jit(solution)/shard_map/all_to_all | solution.py:150
  129.6 8.1 %all-to-all-start.4 = ((f32[8,16,256]{2,1,0:T(8,128)}), f32[8,16,256]{2,1,0:T(8,128)S(1)}, u32[]{:S(2)}, u32[]{:S(2)}) async-start(f32[8,16,256]{2,1,0:T(8,128)} %copy.189), calls=%async_computation.4 | async-start | bytes 262144 | tf_op jit(solution)/shard_map/all_to_all | solution.py:158
  134.0 11.7 %copy-start.1 = (f32[1,128,256]{2,0,1:T(1,128)}, f32[1,128,256]{2,0,1:T(1,128)S(1)}, u32[]{:S(2)}) copy-start(f32[1,128,256]{2,0,1:T(1,128)S(1)} %all_to_all.96) | copy-start | bytes 393220
  137.8 134.5 %all-to-all-start.6 = ((f32[8,16,256]{2,0,1:T(8,128)}), f32[8,16,256]{2,0,1:T(8,128)}, u32[]{:S(2)}, u32[]{:S(2)}) async-start(f32[8,16,256]{2,0,1:T(8,128)} %copy.184), calls=%async_computation.6 | async-start | bytes 262144 | tf_op jit(solution)/shard_map/all_to_all | solution.py:165
  272.2 28.5 %all-to-all-start.1 = ((f32[8,16,256]{2,1,0:T(8,128)}), f32[8,16,256]{2,1,0:T(8,128)S(1)}, u32[]{:S(2)}, u32[]{:S(2)}) async-start(f32[8,16,256]{2,1,0:T(8,128)} %copy.187), calls=%async_computation.1 | async-start | bytes 262144 | tf_op jit(solution)/shard_map/all_to_all | solution.py:151
  288.1 27.0 %copy-start.2 = (f32[1,128,256]{2,0,1:T(1,128)S(1)}, f32[1,128,256]{2,0,1:T(1,128)}, u32[]{:S(2)}) copy-start(f32[1,128,256]{2,0,1:T(1,128)} %copy-done.1) | copy-start | bytes 393220
  288.1 27.0 %slice-start = ((f32[1,64,256]{2,0,1:T(1,128)}), f32[1,63,256]{2,0,1:T(1,128)S(1)}, s32[]{:S(2)}) async-start(f32[1,64,256]{2,0,1:T(1,128)} %copy-done.3), calls=%async_computation.9 | async-start | bytes 129024 | tf_op jit(solution)/shard_map/slice | solution.py:60
  300.7 25.9 %all-to-all-start.7 = ((f32[8,16,256]{2,0,1:T(8,128)}), f32[8,16,256]{2,0,1:T(8,128)S(1)}, u32[]{:S(2)}, u32[]{:S(2)}) async-start(f32[8,16,256]{2,0,1:T(8,128)} %fusion.30), calls=%async_computation.7 | async-start | bytes 262144 | tf_op jit(solution)/shard_map/all_to_all | solution.py:166
  326.6 17.6 %all-to-all-start.2 = ((f32[1,128,256]{2,0,1:T(1,128)}), f32[1,128,256]{2,0,1:T(1,128)S(1)}, u32[]{:S(2)}, u32[]{:S(2)}) async-start(f32[1,128,256]{2,0,1:T(1,128)} %bitcast.24), calls=%async_computation.2 | async-start | bytes 262144 | tf_op jit(solution)/shard_map/all_to_all | solution.py:154
  344.2 18.8 %all-to-all-start.8 = ((f32[128,1,256]{2,1,0:T(1,128)}), f32[128,1,256]{2,1,0:T(1,128)S(1)}, u32[]{:S(2)}, u32[]{:S(2)}) async-start(f32[128,1,256]{2,1,0:T(1,128)} %bitcast.101), calls=%async_computation.8 | async-start | bytes 262144 | tf_op jit(solution)/shard_map/all_to_all | solution.py:169
  362.9 8.1 %all-to-all-start.5 = ((f32[4,2,16,256]{3,2,1,0:T(8,128)}), f32[4,2,16,256]{3,2,1,0:T(8,128)S(1)}, u32[]{:S(2)}, u32[]{:S(2)}) async-start(f32[4,2,16,256]{3,2,1,0:T(8,128)} %pad_maximum_fusion.20), calls=%async_computation.5 | async-start | bytes 262144 | tf_op jit(solution)/shard_map/all_to_all | solution.py:161
  (2 other events, 21.1 us)
